TPU v7x, 32 devices: a whole 2x2x4 slice. The times are simulated.
32 devices in a mesh: section: 2 (over x), dp: 4 (over y, core), expert: 4 (over z).
Axes of the slice: x: 2, y: 2, z: 4, core: 2. Of those that a mesh axis runs over, the one named last changes fastest.
Arguments:
- inbound: bfloat16 [2, 16, 256, 1024], P('section', ('dp', 'expert')), may hold values from -6 to 6
- queued: bfloat16 [16, 256, 1024], P(('dp', 'expert')), may hold values from -6 to 6
- routes: int32 [2, 2, 16, 256, 1], P('section', None, ('dp', 'expert')), may hold values from 0 to 3
- first_gain: float32 [2, 1024], P('section'), may hold values from 0.1 to 1.9
- attention_in: bfloat16 [2, 1024, 1536], P('section', 'dp'), may hold values from -3.1875 to 3.1875
- attention_out: bfloat16 [2, 512, 1024], P('section', 'dp'), may hold values from -0.25 to 0.25
- second_gain: float32 [2, 1024], P('section'), may hold values from 0.1 to 1.9
- router: bfloat16 [2, 1024, 4], P('section'), may hold values from -0.375 to 0.375
- expert_in: bfloat16 [2, 4, 1024, 2048], P('section', 'expert', 'dp'), may hold values from -0.1875 to 0.1875
- expert_out: bfloat16 [2, 4, 2048, 1024], P('section', 'expert', 'dp'), may hold values from -0.125 to 0.125
Outputs:
- section_output: bfloat16 [2, 2, 16, 256, 1024], P('section', None, ('dp', 'expert'))
All inputs are finite; a program needn't handle non-finite values.
Results may differ from a plain program's by a relative error of at most 0.0056.
Values may be sent and summed in bfloat16 or wider, within the bound.
A program may use at most 64 MiB of HBM per device.

v0:
```python
from functools import partial
import jax
import jax.numpy as jnp
from jax import lax
from jax.sharding import PartitionSpec as P

HEAD_DIM = 64
CAP = 16
EPSILON = 1e-06


def shifted(shard, axis, by):
    count = lax.axis_size(axis)
    pairs = [(i, i + by) for i in range(count) if 0 <= i + by < count]
    return lax.ppermute(shard, axis, pairs)


def layer_norm(activations, gain_vector):
    widened = activations.astype(jnp.float32)
    centre = widened - jnp.mean(widened, axis=-1, keepdims=True)
    spread = jnp.mean(centre * centre, axis=-1, keepdims=True)
    return (centre * lax.rsqrt(spread + EPSILON) * gain_vector).astype(jnp.bfloat16)


def build_slots(chosen, expert_count):
    onehot = (chosen[:, None] == jnp.arange(expert_count, dtype=jnp.int32)[None, :]).astype(
        jnp.int32
    )
    before = jnp.cumsum(onehot, axis=0) - onehot
    position = jnp.sum(before * onehot, axis=1)
    retained = position < CAP
    slot_index = chosen * CAP + position
    slot_table = (
        slot_index[:, None] == jnp.arange(expert_count * CAP, dtype=jnp.int32)[None, :]
    ) & retained[:, None]
    return (onehot, slot_table, slot_index, retained)


def attend(tokens, gain_vector, project_in, project_out):
    image_count, token_count, model_width = tokens.shape
    head_width = project_out.shape[0]
    head_count = head_width // HEAD_DIM
    normed = layer_norm(tokens, gain_vector)
    mixed_rows = jnp.dot(
        normed.reshape(image_count * token_count, model_width),
        project_in,
        preferred_element_type=jnp.float32,
    ).astype(jnp.bfloat16)
    mixed_rows = mixed_rows.reshape(image_count, token_count, 3, head_count, HEAD_DIM)
    scores = jnp.einsum(
        "ishd,ithd->ihst",
        mixed_rows[:, :, 0],
        mixed_rows[:, :, 1],
        preferred_element_type=jnp.float32,
    ) * HEAD_DIM ** (-0.5)
    softmax_weights = jax.nn.softmax(scores, axis=-1).astype(jnp.bfloat16)
    context = jnp.einsum(
        "ihst,ithd->ishd", softmax_weights, mixed_rows[:, :, 2], preferred_element_type=jnp.float32
    )
    context = context.astype(jnp.bfloat16).reshape(image_count * token_count, head_width)
    branch = jnp.dot(context, project_out, preferred_element_type=jnp.float32).reshape(
        image_count, token_count, model_width
    )
    return (tokens.astype(jnp.float32) + branch).astype(jnp.bfloat16)


def route_and_mix(residual, chosen, gain_vector, router_cols, own_in, own_out):
    image_count, token_count, model_width = residual.shape
    expert_count = router_cols.shape[1]
    normed = layer_norm(residual, gain_vector)
    logits = jnp.dot(
        normed.reshape(image_count * token_count, model_width),
        router_cols,
        preferred_element_type=jnp.float32,
    ).reshape(image_count, token_count, expert_count)
    onehot, slot_table, slot_index, retained = jax.vmap(
        partial(build_slots, expert_count=expert_count)
    )(chosen)
    gating = jax.nn.sigmoid(jnp.sum(logits * onehot.astype(jnp.float32), axis=-1))
    outgoing = jnp.einsum(
        "isk,isd->ikd", slot_table.astype(jnp.bfloat16), normed, preferred_element_type=jnp.float32
    ).astype(jnp.bfloat16)
    outgoing = outgoing.reshape(image_count, expert_count, CAP, model_width)
    arrived = lax.all_to_all(outgoing, "expert", split_axis=1, concat_axis=0, tiled=True)
    flat_rows = arrived.reshape(-1, model_width)
    hidden = jax.nn.gelu(
        jnp.dot(flat_rows, own_in, preferred_element_type=jnp.float32), approximate=False
    ).astype(jnp.bfloat16)
    answer = jnp.dot(hidden, own_out, preferred_element_type=jnp.float32).astype(jnp.bfloat16)
    answered = lax.all_to_all(
        answer.reshape(arrived.shape), "expert", split_axis=0, concat_axis=1, tiled=True
    )
    answered = answered.reshape(image_count, expert_count * CAP, model_width)
    combined = jnp.einsum(
        "isk,ikd->isd",
        slot_table.astype(jnp.bfloat16),
        answered,
        preferred_element_type=jnp.float32,
    )
    return (residual.astype(jnp.float32) + gating[:, :, None] * combined).astype(jnp.bfloat16)


def per_device(
    inbound,
    queued,
    routes,
    first_gain,
    attention_in,
    attention_out,
    second_gain,
    router,
    expert_in,
    expert_out,
):
    section_index = lax.axis_index("section")
    chosen = routes[0, :, :, :, 0]
    full_in, full_out = (
        lax.all_gather(attention_in, "dp", axis=1, tiled=True),
        lax.all_gather(attention_out, "dp", axis=1, tiled=True),
    )
    first_mixed = attend(inbound[0], first_gain[0], full_in[0], full_out[0])
    own_in, own_out = (
        lax.all_gather(expert_in[:, 0], "dp", axis=1, tiled=True),
        lax.all_gather(expert_out[:, 0], "dp", axis=1, tiled=True),
    )
    first_tick = route_and_mix(
        first_mixed, chosen[0], second_gain[0], router[0], own_in[0], own_out[0]
    )
    arrived = shifted(first_tick, "section", 1)
    entering = jnp.where(section_index == 0, queued, arrived)
    second_mixed = attend(entering, first_gain[0], full_in[0], full_out[0])
    second_tick = route_and_mix(
        second_mixed, chosen[1], second_gain[0], router[0], own_in[0], own_out[0]
    )
    return jnp.stack([first_tick, second_tick])[None]


def solution(mesh):
    in_specs = (
        P("section", ("dp", "expert"), None, None),
        P(("dp", "expert"), None, None),
        P("section", None, ("dp", "expert"), None, None),
        P("section", None),
        P("section", "dp", None),
        P("section", "dp", None),
        P("section", None),
        P("section", None, None),
        P("section", "expert", "dp", None),
        P("section", "expert", "dp", None),
    )
    out_specs = P("section", None, ("dp", "expert"), None, None)
    return jax.shard_map(
        per_device, mesh=mesh, in_specs=in_specs, out_specs=out_specs, check_vma=False
    )
```

profile of v0, /device:TPU:0, one launch (start us, length us, event | category | flops | bytes accessed | tf_op | source)
XLA Modules:
  0.0 201.7 jit_solution(5057114900987125693)
XLA Ops:
  9.4 1.2 reduce-window.14
  11.1 1.2 reduce-window.16
  13.0 27.2 %all-gather.7.cloned.1.call-done = bf16[1,1024,1536]{2,1,0:T(8,128)(2,1)} async-done(((bf16[1,256,1536]{2,1,0:T(8,128)(2,1)}), bf16[1,1024,1536]{2,1,0:T(8,128)(2,1)}) %all-gather.7.cloned.1.call-update) | async-done | bytes 3145744 | tf_op jit(solution)/shard_map/all_gather | solution.py:118
  40.2 3.0 %fusion.14 = bf16[256,1536]{1,0:T(8,128)(2,1)S(1)} fusion(bf16[1,1024,1536]{2,1,0:T(8,128)(2,1)} %all-gather.7.cloned.1.call-done, bf16[1,1,256,1024]{3,2,1,0:T(8,128)(2,1)S(1)} %copy-done.1, f32[1024]{0:T(1024)S(1)} %bitcast.238, f32[256]{0:T(256)S(1)} %add_rsqrt_fusion.3, f32[256]{0:T(256)S(1)} %broadcast_multiply_fusion.3), kind=kOutput, calls=%fused_computation.14 | convolution fusion | flops 807010304 | bytes 4462592 | tf_op jit(solution)/shard_map/dot_general | solution.py:44
  44.3 1.1 convolution_convert_fusion.1
  45.4 13.1 %all-gather.9.cloned.1.call-done = bf16[1,512,1024]{2,1,0:T(8,128)(2,1)} async-done(((bf16[1,128,1024]{2,1,0:T(8,128)(2,1)}), bf16[1,512,1024]{2,1,0:T(8,128)(2,1)}) %all-gather.9.cloned.1.call-update) | async-done | bytes 1048592 | tf_op jit(solution)/shard_map/all_gather | solution.py:119
  58.5 1.8 convert_reduce_fusion.3
  61.9 4.6 %all-to-all-start = ((bf16[1,4,16,1024]{3,2,0,1:T(8,128)(2,1)}), bf16[1,4,16,1024]{3,2,0,1:T(8,128)(2,1)S(1)}, u32[]{:S(2)}, u32[]{:S(2)}) async-start(bf16[1,4,16,1024]{3,2,0,1:T(8,128)(2,1)} %bitcast.22), calls=%async_computation | async-start | bytes 262144 | tf_op jit(solution)/shard_map/all_to_all | solution.py:84
  67.0 5.8 %all-to-all-done = bf16[1,4,16,1024]{3,2,0,1:T(8,128)(2,1)S(1)} async-done(((bf16[1,4,16,1024]{3,2,0,1:T(8,128)(2,1)}), bf16[1,4,16,1024]{3,2,0,1:T(8,128)(2,1)S(1)}, u32[]{:S(2)}, u32[]{:S(2)}) %all-to-all-start) | async-done | bytes 131104 | tf_op jit(solution)/shard_map/all_to_all | solution.py:84
  72.8 21.8 %all-gather.11.cloned.1.call-done = bf16[1,1,1024,2048]{3,2,1,0:T(8,128)(2,1)} async-done(((bf16[1,1,256,2048]{3,2,1,0:T(8,128)(2,1)}), bf16[1,1,1024,2048]{3,2,1,0:T(8,128)(2,1)}) %all-gather.11.cloned.1.call-update) | async-done | bytes 4194320 | tf_op jit(solution)/shard_map/all_gather | solution.py:123
  94.6 35.9 %all-gather.13.cloned.1.call-done = bf16[1,1,2048,1024]{3,2,1,0:T(8,128)(2,1)} async-done(((bf16[1,1,512,1024]{3,2,1,0:T(8,128)(2,1)}), bf16[1,1,2048,1024]{3,2,1,0:T(8,128)(2,1)}) %all-gather.13.cloned.1.call-update) | async-done | bytes 4194320 | tf_op jit(solution)/shard_map/all_gather | solution.py:124
  130.5 6.8 %fusion.34 = bf16[64,1024]{1,0:T(8,128)(2,1)} fusion(bf16[1,1,2048,1024]{3,2,1,0:T(8,128)(2,1)} %all-gather.13.cloned.1.call-done, bf16[64,1024]{1,0:T(8,128)(2,1)S(1)} %bitcast.224, bf16[1,1,1024,2048]{3,2,1,0:T(8,128)(2,1)} %all-gather.11.cloned.1.call-done), kind=kOutput, calls=%fused_computation.55 | convolution fusion | flops 545456128 | bytes 8650752 | tf_op jit(solution)/shard_map/dot_general | solution.py:89
  137.3 4.6 %all-to-all-start.1 = ((bf16[4,1,16,1024]{3,2,1,0:T(8,128)(2,1)}), bf16[4,1,16,1024]{3,2,1,0:T(8,128)(2,1)S(1)}, u32[]{:S(2)}, u32[]{:S(2)}) async-start(bf16[4,1,16,1024]{3,2,1,0:T(8,128)(2,1)} %bitcast.27), calls=%async_computation.1 | async-start | bytes 262144 | tf_op jit(solution)/shard_map/all_to_all | solution.py:90
  142.0 6.3 %all-to-all-done.1 = bf16[4,1,16,1024]{3,2,1,0:T(8,128)(2,1)S(1)} async-done(((bf16[4,1,16,1024]{3,2,1,0:T(8,128)(2,1)}), bf16[4,1,16,1024]{3,2,1,0:T(8,128)(2,1)S(1)}, u32[]{:S(2)}, u32[]{:S(2)}) %all-to-all-start.1) | async-done | bytes 131104 | tf_op jit(solution)/shard_map/all_to_all | solution.py:90
  148.6 3.7 %collective-permute-start = (bf16[1,256,1024]{2,1,0:T(8,128)(2,1)S(1)}, bf16[1,256,1024]{2,1,0:T(8,128)(2,1)S(1)}, u32[]{:S(2)}, u32[]{:S(2)}) collective-permute-start(bf16[1,256,1024]{2,1,0:T(8,128)(2,1)S(1)} %bitcast.216), channel_id=1, source_target_pairs={{0,16},{1,17},{2,18},{3,19},{4,20},{5,21},{6,22},{7,23},{8,24},{9,... | collective-permute-start | bytes 1572872 | tf_op jit(solution)/shard_map/ppermute | solution.py:15
  152.4 9.5 %collective-permute-done = bf16[1,256,1024]{2,1,0:T(8,128)(2,1)S(1)} collective-permute-done((bf16[1,256,1024]{2,1,0:T(8,128)(2,1)S(1)}, bf16[1,256,1024]{2,1,0:T(8,128)(2,1)S(1)}, u32[]{:S(2)}, u32[]{:S(2)}) %collective-permute-start) | collective-permute-done | bytes 524320 | tf_op jit(solution)/shard_map/ppermute | solution.py:15
  162.5 1.1 fusion.17
  164.7 1.1 convolution_convert_fusion
  167.9 3.9 %all-to-all-start.2 = ((bf16[1,4,16,1024]{3,2,0,1:T(8,128)(2,1)}), bf16[1,4,16,1024]{3,2,0,1:T(8,128)(2,1)S(1)}, u32[]{:S(2)}, u32[]{:S(2)}) async-start(bf16[1,4,16,1024]{3,2,0,1:T(8,128)(2,1)} %bitcast.48), calls=%async_computation.2 | async-start | bytes 262144 | tf_op jit(solution)/shard_map/all_to_all | solution.py:84
  172.1 5.7 %all-to-all-done.2 = bf16[1,4,16,1024]{3,2,0,1:T(8,128)(2,1)S(1)} async-done(((bf16[1,4,16,1024]{3,2,0,1:T(8,128)(2,1)}), bf16[1,4,16,1024]{3,2,0,1:T(8,128)(2,1)S(1)}, u32[]{:S(2)}, u32[]{:S(2)}) %all-to-all-start.2) | async-done | bytes 131104 | tf_op jit(solution)/shard_map/all_to_all | solution.py:84
  177.7 6.8 %fusion.37 = bf16[64,1024]{1,0:T(8,128)(2,1)} fusion(bf16[1,1,2048,1024]{3,2,1,0:T(8,128)(2,1)} %all-gather.13.cloned.1.call-done, bf16[64,1024]{1,0:T(8,128)(2,1)S(1)} %bitcast.225, bf16[1,1,1024,2048]{3,2,1,0:T(8,128)(2,1)} %all-gather.11.cloned.1.call-done), kind=kOutput, calls=%fused_computation.56 | convolution fusion | flops 545456128 | bytes 8650752 | tf_op jit(solution)/shard_map/dot_general | solution.py:89
  184.5 3.3 %all-to-all-start.3 = ((bf16[4,1,16,1024]{3,2,1,0:T(8,128)(2,1)}), bf16[4,1,16,1024]{3,2,1,0:T(8,128)(2,1)S(1)}, u32[]{:S(2)}, u32[]{:S(2)}) async-start(bf16[4,1,16,1024]{3,2,1,0:T(8,128)(2,1)} %bitcast.51), calls=%async_computation.3 | async-start | bytes 262144 | tf_op jit(solution)/shard_map/all_to_all | solution.py:90
  187.8 5.9 %all-to-all-done.3 = bf16[4,1,16,1024]{3,2,1,0:T(8,128)(2,1)S(1)} async-done(((bf16[4,1,16,1024]{3,2,1,0:T(8,128)(2,1)}), bf16[4,1,16,1024]{3,2,1,0:T(8,128)(2,1)S(1)}, u32[]{:S(2)}, u32[]{:S(2)}) %all-to-all-start.3) | async-done | bytes 131104 | tf_op jit(solution)/shard_map/all_to_all | solution.py:90
  194.1 1.1 maximum_bitcast_fusion
  (80 shorter events, 11.9 us)
Async XLA Ops:
  6.5 60.2 %copy-start = (bf16[1,1024,4]{1,2,0:T(4,128)(2,1)S(1)}, bf16[1,1024,4]{1,2,0:T(4,128)(2,1)}, u32[]{:S(2)}) copy-start(bf16[1,1024,4]{1,2,0:T(4,128)(2,1)} %param.17) | copy-start | bytes 24580
  6.5 2.8 %copy-start.4 = (s32[1,2,1,256,1]{3,4,2,1,0:T(1,128)S(1)}, s32[1,2,1,256,1]{3,4,2,1,0:T(1,128)}, u32[]{:S(2)}) copy-start(s32[1,2,1,256,1]{3,4,2,1,0:T(1,128)} %param.12) | copy-start | bytes 6148
  6.5 6.0 %copy-start.1 = (bf16[1,1,256,1024]{3,2,1,0:T(8,128)(2,1)S(1)}, bf16[1,1,256,1024]{3,2,1,0:T(8,128)(2,1)}, u32[]{:S(2)}) copy-start(bf16[1,1,256,1024]{3,2,1,0:T(8,128)(2,1)} %param.10) | copy-start | bytes 1572868
  6.5 33.7 %copy-start.7 = (f32[1,1024]{1,0:T(1,128)S(1)}, f32[1,1024]{1,0:T(1,128)}, u32[]{:S(2)}) copy-start(f32[1,1024]{1,0:T(1,128)} %param.13) | copy-start | bytes 12292
  6.5 33.7 %all-gather.7.cloned.1.call-start = ((), (), s32[]{:S(2)}) async-start(), calls=%async_computation.4 | async-start | bytes 3932160 | tf_op jit(solution)/shard_map/all_gather | solution.py:118
  7.3 51.2 %all-gather.9.cloned.1.call-start = ((), (), s32[]{:S(2)}) async-start(), calls=%async_computation.5 | async-start | bytes 1310720 | tf_op jit(solution)/shard_map/all_gather | solution.py:119
  8.0 86.6 %all-gather.11.cloned.1.call-start = ((), (), s32[]{:S(2)}) async-start(), calls=%async_computation.6 | async-start | bytes 5242880 | tf_op jit(solution)/shard_map/all_gather | solution.py:123
  8.8 121.8 %all-gather.13.cloned.1.call-start = ((), (), s32[]{:S(2)}) async-start(), calls=%async_computation.7 | async-start | bytes 5242880 | tf_op jit(solution)/shard_map/all_gather | solution.py:124
  45.4 15.2 %copy-start.3 = (f32[1,1024]{1,0:T(1,128)S(1)}, f32[1,1024]{1,0:T(1,128)}, u32[]{:S(2)}) copy-start(f32[1,1024]{1,0:T(1,128)} %param.16) | copy-start | bytes 12292
  61.9 10.9 %all-to-all-start = ((bf16[1,4,16,1024]{3,2,0,1:T(8,128)(2,1)}), bf16[1,4,16,1024]{3,2,0,1:T(8,128)(2,1)S(1)}, u32[]{:S(2)}, u32[]{:S(2)}) async-start(bf16[1,4,16,1024]{3,2,0,1:T(8,128)(2,1)} %bitcast.22), calls=%async_computation | async-start | bytes 262144 | tf_op jit(solution)/shard_map/all_to_all | solution.py:84
  130.5 31.4 %copy-start.2 = (bf16[1,256,1024]{2,1,0:T(8,128)(2,1)S(1)}, bf16[1,256,1024]{2,1,0:T(8,128)(2,1)}, u32[]{:S(2)}) copy-start(bf16[1,256,1024]{2,1,0:T(8,128)(2,1)} %param.11) | copy-start | bytes 1572868
  137.3 10.9 %all-to-all-start.1 = ((bf16[4,1,16,1024]{3,2,1,0:T(8,128)(2,1)}), bf16[4,1,16,1024]{3,2,1,0:T(8,128)(2,1)S(1)}, u32[]{:S(2)}, u32[]{:S(2)}) async-start(bf16[4,1,16,1024]{3,2,1,0:T(8,128)(2,1)} %bitcast.27), calls=%async_computation.1 | async-start | bytes 262144 | tf_op jit(solution)/shard_map/all_to_all | solution.py:90
  148.3 14.2 %copy-start.5 = (bf16[1,1024,1536]{2,1,0:T(8,128)(2,1)S(1)}, bf16[1,1024,1536]{2,1,0:T(8,128)(2,1)}, u32[]{:S(2)}) copy-start(bf16[1,1024,1536]{2,1,0:T(8,128)(2,1)} %all-gather.7.cloned.1.call-done) | copy-start | bytes 9437188
  148.6 13.3 %collective-permute-start = (bf16[1,256,1024]{2,1,0:T(8,128)(2,1)S(1)}, bf16[1,256,1024]{2,1,0:T(8,128)(2,1)S(1)}, u32[]{:S(2)}, u32[]{:S(2)}) collective-permute-start(bf16[1,256,1024]{2,1,0:T(8,128)(2,1)S(1)} %bitcast.216), channel_id=1, source_target_pairs={{0,16},{1,17},{2,18},{3,19},{4,20},{5,21},{6,22},{7,23},{8,24},{9,... | collective-permute-start | bytes 1572872 | tf_op jit(solution)/shard_map/ppermute | solution.py:15
  164.7 1.2 copy-start.6
  167.9 9.8 %all-to-all-start.2 = ((bf16[1,4,16,1024]{3,2,0,1:T(8,128)(2,1)}), bf16[1,4,16,1024]{3,2,0,1:T(8,128)(2,1)S(1)}, u32[]{:S(2)}, u32[]{:S(2)}) async-start(bf16[1,4,16,1024]{3,2,0,1:T(8,128)(2,1)} %bitcast.48), calls=%async_computation.2 | async-start | bytes 262144 | tf_op jit(solution)/shard_map/all_to_all | solution.py:84
  184.5 9.2 %all-to-all-start.3 = ((bf16[4,1,16,1024]{3,2,1,0:T(8,128)(2,1)}), bf16[4,1,16,1024]{3,2,1,0:T(8,128)(2,1)S(1)}, u32[]{:S(2)}, u32[]{:S(2)}) async-start(bf16[4,1,16,1024]{3,2,1,0:T(8,128)(2,1)} %bitcast.51), calls=%async_computation.3 | async-start | bytes 262144 | tf_op jit(solution)/shard_map/all_to_all | solution.py:90
Sparse Core Ops, SparseCore 0:
  8.9 31.2 all-gather.6
  41.8 16.7 all-gather.8
  60.1 34.4 all-gather.10
  96.0 34.4 all-gather.12
where the time goes:
time: 202 us
  waiting for transfers between devices  134 us (66%)
  matrix products  26.9 us (13%)
  starting transfers between devices  20.3 us (10%)
  between operations  13.3 us (7%)
  other arithmetic  5.87 us (3%)
    all_gather x1, waiting for transfers between devices, per_device(): lax.all_gather(expert_out[:, 0], 'dp', axis=1, tiled=True)  35.9 us
    all_gather x1, waiting for transfers between devices, per_device(): lax.all_gather(attention_in, 'dp', axis=1, tiled=True)  27.2 us
    all_gather x1, waiting for transfers between devices, per_device(): lax.all_gather(expert_in[:, 0], 'dp', axis=1, tiled=True)  21.8 us
    dot_general x2, matrix products, route_and_mix(): jnp.dot(hidden, own_out, preferred_element_type=jnp.float32)  13.6 us
    all_gather x1, waiting for transfers between devices, per_device(): lax.all_gather(attention_out, 'dp', axis=1, tiled=True)  13.1 us
    all_to_all x2, waiting for transfers between devices, route_and_mix(): lax.all_to_all(answer.reshape(arrived.shape), 'expert', split_axis=0, con...  12.2 us
    all_to_all x2, waiting for transfers between devices, route_and_mix(): lax.all_to_all(outgoing, 'expert', split_axis=1, concat_axis=0, tiled=True)  11.5 us
    ppermute x1, waiting for transfers between devices, shifted(): return lax.ppermute(shard, axis, pairs)  9.51 us
  transfers between devices with their start and end apart: 9, of which 9 were waited for; matrix products, arithmetic and copies ran while one was open for 6% of the time, Pallas kernels for 0%

commit v1 on v0

--- a/solution.py
+++ b/solution.py
@@ -7,6 +7,18 @@
 HEAD_DIM = 64
 CAP = 16
 EPSILON = 1e-06
+
+
+def gather_by_bits(x, axis, dim):
+    ways, here = (lax.axis_size(axis), lax.axis_index(axis))
+    grown, reach = (x, 1)
+    while reach < ways:
+        theirs = lax.ppermute(grown, axis, [(d, d ^ reach) for d in range(ways)])
+        mine_first = jnp.concatenate([grown, theirs], axis=dim)
+        theirs_first = jnp.concatenate([theirs, grown], axis=dim)
+        grown = jnp.where(here & reach == 0, mine_first, theirs_first)
+        reach = 2 * reach
+    return grown
 
 
 def shifted(shard, axis, by):
@@ -121,7 +133,7 @@
     first_mixed = attend(inbound[0], first_gain[0], full_in[0], full_out[0])
     own_in, own_out = (
         lax.all_gather(expert_in[:, 0], "dp", axis=1, tiled=True),
-        lax.all_gather(expert_out[:, 0], "dp", axis=1, tiled=True),
+        gather_by_bits(expert_out[:, 0], "dp", 1),
     )
     first_tick = route_and_mix(
         first_mixed, chosen[0], second_gain[0], router[0], own_in[0], own_out[0]

time: 202 us -> 192 us (0.950)
  waiting for transfers between devices: 134 us -> 110 us
  matrix products: 26.9 us -> 32.1 us
  other arithmetic: 5.87 us -> 10.6 us
  starting transfers between devices: 20.3 us -> 23.3 us
    all_gather x1 -> x0, waiting for transfers between devices: 35.9 us -> none  [per_device(): lax.all_gather(expert_out[:, 0], 'dp', axis=1, tiled=True)]
    all_gather x1, waiting for transfers between devices: 27.2 us -> 39 us  [per_device(): lax.all_gather(attention_in, 'dp', axis=1, tiled=True)]
    select_n x0 -> x2, other arithmetic: none -> 4.76 us  [gather_by_bits(): grown = jnp.where(here & reach == 0, mine_first, theirs_first)]
    ppermute x0 -> x2, starting transfers between devices: none -> 3.07 us  [gather_by_bits(): theirs = lax.ppermute(grown, axis, [(d, d ^ reach) for d in range(ways)])]
    all_gather x1, waiting for transfers between devices: 13.1 us -> 16.1 us  [per_device(): lax.all_gather(attention_out, 'dp', axis=1, tiled=True)]
    dot_general x2, matrix products: 13.6 us -> 15.7 us  [route_and_mix(): jnp.dot(hidden, own_out, preferred_element_type=jnp.float32)]
    all_to_all x2, waiting for transfers between devices: 11.5 us -> 9.36 us  [route_and_mix(): lax.all_to_all(outgoing, 'expert', split_axis=1, concat_axis=0, tiled=True)]
  transfers between devices with their start and end apart: 9 -> 10, of which waited for: 9 -> 8; matrix products, arithmetic and copies ran while one was open for 6% -> 11% of each run, Pallas kernels for 0% -> 0%
where the time goes in v1:
time: 192 us
  waiting for transfers between devices  110 us (57%)
  matrix products  32.1 us (17%)
  starting transfers between devices  23.3 us (12%)
  between operations  13.4 us (7%)
  other arithmetic  10.6 us (6%)
  local copies, waits for them, and re-layouts  2.27 us (1%)
    all_gather x1, waiting for transfers between devices, per_device(): lax.all_gather(attention_in, 'dp', axis=1, tiled=True)  39 us
    all_gather x1, waiting for transfers between devices, per_device(): lax.all_gather(expert_in[:, 0], 'dp', axis=1, tiled=True)  21.7 us
    all_gather x1, waiting for transfers between devices, per_device(): lax.all_gather(attention_out, 'dp', axis=1, tiled=True)  16.1 us
    dot_general x2, matrix products, route_and_mix(): jnp.dot(hidden, own_out, preferred_element_type=jnp.float32)  15.7 us
    all_to_all x2, waiting for transfers between devices, route_and_mix(): lax.all_to_all(answer.reshape(arrived.shape), 'expert', split_axis=0, con...  12.2 us
    ppermute x1, waiting for transfers between devices, shifted(): return lax.ppermute(shard, axis, pairs)  9.51 us
    all_to_all x2, waiting for transfers between devices, route_and_mix(): lax.all_to_all(outgoing, 'expert', split_axis=1, concat_axis=0, tiled=True)  9.36 us
    all_to_all x2, starting transfers between devices, route_and_mix(): lax.all_to_all(outgoing, 'expert', split_axis=1, concat_axis=0, tiled=True)  8.49 us
  transfers between devices with their start and end apart: 10, of which 8 were waited for; matrix products, arithmetic and copies ran while one was open for 11% of the time, Pallas kernels for 0%

profile of v1, /device:TPU:0, one launch (start us, length us, event | category | flops | bytes accessed | tf_op | source)
XLA Modules:
  0.0 191.6 jit_solution(7888486895253215492)
XLA Ops:
  9.3 1.2 reduce-window.14
  13.2 2.4 %maximum_select_fusion.2 = bf16[1,1024,1024]{2,1,0:T(8,128)(2,1)} fusion(bf16[1,512,1024]{2,1,0:T(8,128)(2,1)S(1)} %collective-permute-done, bf16[1,512,1024]{2,1,0:T(8,128)(2,1)S(1)} %bitcast.212, pred[]{:T(512)S(6)} %eq.160), kind=kLoop, calls=%fused_computation.14 | loop fusion | flops 9437184 | bytes 4194305 | tf_op jit(solution)/shard_map/jit(_where)/select_n | solution.py:19
  15.6 2.5 %collective-permute-start.1 = (bf16[1,1024,1024]{2,1,0:T(8,128)(2,1)}, bf16[1,1024,1024]{2,1,0:T(8,128)(2,1)}, u32[]{:S(2)}, u32[]{:S(2)}) collective-permute-start(bf16[1,1024,1024]{2,1,0:T(8,128)(2,1)} %maximum_select_fusion.2), channel_id=1, source_target_pairs={{0,8},{4,12},{8,0},{12,4},{1,9},{5,13},{9,1},{13,5},{2,10},{6,14},... | collective-permute-start | bytes 6291464 | tf_op jit(solution)/shard_map/ppermute | solution.py:16
  18.1 39.0 %all-gather.5.cloned.1.call-done = bf16[1,1024,1536]{2,1,0:T(8,128)(2,1)} async-done(((bf16[1,256,1536]{2,1,0:T(8,128)(2,1)}), bf16[1,1024,1536]{2,1,0:T(8,128)(2,1)}) %all-gather.5.cloned.1.call-update) | async-done | bytes 3145744 | tf_op jit(solution)/shard_map/all_gather | solution.py:130
  57.2 3.0 %fusion.10 = bf16[256,1536]{1,0:T(8,128)(2,1)S(1)} fusion(bf16[1,1024,1536]{2,1,0:T(8,128)(2,1)} %all-gather.5.cloned.1.call-done, bf16[1,1,256,1024]{3,2,1,0:T(8,128)(2,1)S(1)} %copy-done.3, f32[1024]{0:T(1024)S(1)} %bitcast.237, f32[256]{0:T(256)S(1)} %add_rsqrt_fusion.3, f32[256]{0:T(256)S(1)} %broadcast_multiply_fusion.3), kind=kOutput, calls=%fused_computation.11 | convolution fusion | flops 807010304 | bytes 4462592 | tf_op jit(solution)/shard_map/dot_general | solution.py:56
  61.3 1.9 %fusion.254 = f32[8,256]{1,0:T(8,128)S(1)} fusion(bf16[1,256,3,8,64]{1,4,3,2,0:T(8,128)(2,1)} %bitcast.217), kind=kOutput, calls=%fused_computation.313 | convolution fusion | flops 68681984 | bytes 532480 | tf_op jit(solution)/shard_map/sub | solution.py:68
  63.2 1.8 convolution_convert_fusion.1
  65.0 16.1 %all-gather.7.cloned.1.call-done = bf16[1,512,1024]{2,1,0:T(8,128)(2,1)} async-done(((bf16[1,128,1024]{2,1,0:T(8,128)(2,1)}), bf16[1,512,1024]{2,1,0:T(8,128)(2,1)}) %all-gather.7.cloned.1.call-update) | async-done | bytes 1048592 | tf_op jit(solution)/shard_map/all_gather | solution.py:131
  81.1 1.9 convert_reduce_fusion.3
  84.6 4.6 %all-to-all-start = ((bf16[1,4,16,1024]{3,2,0,1:T(8,128)(2,1)}), bf16[1,4,16,1024]{3,2,0,1:T(8,128)(2,1)S(1)}, u32[]{:S(2)}, u32[]{:S(2)}) async-start(bf16[1,4,16,1024]{3,2,0,1:T(8,128)(2,1)} %bitcast.22), calls=%async_computation | async-start | bytes 262144 | tf_op jit(solution)/shard_map/all_to_all | solution.py:96
  89.2 2.3 %maximum_select_fusion.1 = bf16[1024,1024]{1,0:T(8,128)(2,1)} fusion(bf16[512,1024]{1,0:T(8,128)(2,1)S(1)} %bitcast.214, bf16[512,1024]{1,0:T(8,128)(2,1)S(1)} %bitcast.213, pred[]{:T(512)S(6)} %eq.160), kind=kLoop, calls=%fused_computation.13 | loop fusion | flops 9437184 | bytes 4194305 | tf_op jit(solution)/shard_map/jit(_where)/select_n | solution.py:19
  91.8 3.7 %all-to-all-done = bf16[1,4,16,1024]{3,2,0,1:T(8,128)(2,1)S(1)} async-done(((bf16[1,4,16,1024]{3,2,0,1:T(8,128)(2,1)}), bf16[1,4,16,1024]{3,2,0,1:T(8,128)(2,1)S(1)}, u32[]{:S(2)}, u32[]{:S(2)}) %all-to-all-start) | async-done | bytes 131104 | tf_op jit(solution)/shard_map/all_to_all | solution.py:96
  95.5 21.7 %all-gather.9.cloned.1.call-done = bf16[1,1,1024,2048]{3,2,1,0:T(8,128)(2,1)} async-done(((bf16[1,1,256,2048]{3,2,1,0:T(8,128)(2,1)}), bf16[1,1,1024,2048]{3,2,1,0:T(8,128)(2,1)}) %all-gather.9.cloned.1.call-update) | async-done | bytes 4194320 | tf_op jit(solution)/shard_map/all_gather | solution.py:135
  117.2 8.5 %convolution_convert_fusion.4 = bf16[64,1024]{1,0:T(8,128)(2,1)} fusion(bf16[1024,1024]{1,0:T(8,128)(2,1)} %bitcast.28, bf16[1024,1024]{1,0:T(8,128)(2,1)} %maximum_select_fusion.1, pred[]{:T(512)S(6)} %eq.159, bf16[64,1024]{1,0:T(8,128)(2,1)S(1)} %bitcast.223, bf16[1,1,1024,2048]{3,2,1,0:T(8,128)(2,1)} %all-gather.9.cloned.1.call-done), kind=kOutput, calls=%fused_computation.56 | convolution fusion | flops 564330496 | bytes 8650753 | tf_op jit(solution)/shard_map/dot_general | solution.py:101
  125.7 4.6 %all-to-all-start.1 = ((bf16[4,1,16,1024]{3,2,1,0:T(8,128)(2,1)}), bf16[4,1,16,1024]{3,2,1,0:T(8,128)(2,1)S(1)}, u32[]{:S(2)}, u32[]{:S(2)}) async-start(bf16[4,1,16,1024]{3,2,1,0:T(8,128)(2,1)} %bitcast.30), calls=%async_computation.1 | async-start | bytes 262144 | tf_op jit(solution)/shard_map/all_to_all | solution.py:102
  130.3 6.3 %all-to-all-done.1 = bf16[4,1,16,1024]{3,2,1,0:T(8,128)(2,1)S(1)} async-done(((bf16[4,1,16,1024]{3,2,1,0:T(8,128)(2,1)}), bf16[4,1,16,1024]{3,2,1,0:T(8,128)(2,1)S(1)}, u32[]{:S(2)}, u32[]{:S(2)}) %all-to-all-start.1) | async-done | bytes 131104 | tf_op jit(solution)/shard_map/all_to_all | solution.py:102
  137.0 3.7 %collective-permute-start.2 = (bf16[1,256,1024]{2,1,0:T(8,128)(2,1)S(1)}, bf16[1,256,1024]{2,1,0:T(8,128)(2,1)S(1)}, u32[]{:S(2)}, u32[]{:S(2)}) collective-permute-start(bf16[1,256,1024]{2,1,0:T(8,128)(2,1)S(1)} %bitcast.215), channel_id=1, source_target_pairs={{0,16},{1,17},{2,18},{3,19},{4,20},{5,21},{6,22},{7,23},{8,24},{9,... | collective-permute-start | bytes 1572872 | tf_op jit(solution)/shard_map/ppermute | solution.py:27
  140.7 9.5 %collective-permute-done.2 = bf16[1,256,1024]{2,1,0:T(8,128)(2,1)S(1)} collective-permute-done((bf16[1,256,1024]{2,1,0:T(8,128)(2,1)S(1)}, bf16[1,256,1024]{2,1,0:T(8,128)(2,1)S(1)}, u32[]{:S(2)}, u32[]{:S(2)}) %collective-permute-start.2) | collective-permute-done | bytes 524320 | tf_op jit(solution)/shard_map/ppermute | solution.py:27
  154.1 1.8 convert_reduce_fusion.1
  157.4 3.9 %all-to-all-start.2 = ((bf16[1,4,16,1024]{3,2,0,1:T(8,128)(2,1)}), bf16[1,4,16,1024]{3,2,0,1:T(8,128)(2,1)S(1)}, u32[]{:S(2)}, u32[]{:S(2)}) async-start(bf16[1,4,16,1024]{3,2,0,1:T(8,128)(2,1)} %bitcast.51), calls=%async_computation.2 | async-start | bytes 262144 | tf_op jit(solution)/shard_map/all_to_all | solution.py:96
  161.5 5.7 %all-to-all-done.2 = bf16[1,4,16,1024]{3,2,0,1:T(8,128)(2,1)S(1)} async-done(((bf16[1,4,16,1024]{3,2,0,1:T(8,128)(2,1)}), bf16[1,4,16,1024]{3,2,0,1:T(8,128)(2,1)S(1)}, u32[]{:S(2)}, u32[]{:S(2)}) %all-to-all-start.2) | async-done | bytes 131104 | tf_op jit(solution)/shard_map/all_to_all | solution.py:96
  167.2 7.3 %convolution_convert_fusion.2 = bf16[64,1024]{1,0:T(8,128)(2,1)} fusion(bf16[1024,1024]{1,0:T(8,128)(2,1)} %bitcast.28, bf16[1024,1024]{1,0:T(8,128)(2,1)S(1)} %copy-done.2, pred[]{:T(512)S(6)} %eq.159, bf16[64,1024]{1,0:T(8,128)(2,1)S(1)} %bitcast.224, bf16[1,1,1024,2048]{3,2,1,0:T(8,128)(2,1)} %all-gather.9.cloned.1.call-done), kind=kOutput, calls=%fused_computation.54 | convolution fusion | flops 564330496 | bytes 8650753 | tf_op jit(solution)/shard_map/dot_general | solution.py:101
  174.5 3.3 %all-to-all-start.3 = ((bf16[4,1,16,1024]{3,2,1,0:T(8,128)(2,1)}), bf16[4,1,16,1024]{3,2,1,0:T(8,128)(2,1)S(1)}, u32[]{:S(2)}, u32[]{:S(2)}) async-start(bf16[4,1,16,1024]{3,2,1,0:T(8,128)(2,1)} %bitcast.54), calls=%async_computation.3 | async-start | bytes 262144 | tf_op jit(solution)/shard_map/all_to_all | solution.py:102
  177.8 5.9 %all-to-all-done.3 = bf16[4,1,16,1024]{3,2,1,0:T(8,128)(2,1)S(1)} async-done(((bf16[4,1,16,1024]{3,2,1,0:T(8,128)(2,1)}), bf16[4,1,16,1024]{3,2,1,0:T(8,128)(2,1)S(1)}, u32[]{:S(2)}, u32[]{:S(2)}) %all-to-all-start.3) | async-done | bytes 131104 | tf_op jit(solution)/shard_map/all_to_all | solution.py:102
  (91 shorter events, 15.7 us)
Async XLA Ops:
  6.5 85.0 %copy-start = (bf16[1,1024,4]{1,2,0:T(4,128)(2,1)S(1)}, bf16[1,1024,4]{1,2,0:T(4,128)(2,1)}, u32[]{:S(2)}) copy-start(bf16[1,1024,4]{1,2,0:T(4,128)(2,1)} %param.17) | copy-start | bytes 24580
  6.5 2.2 %copy-start.1 = (bf16[1,1,512,1024]{3,2,1,0:T(8,128)(2,1)S(1)}, bf16[1,1,512,1024]{3,2,1,0:T(8,128)(2,1)}, u32[]{:S(2)}) copy-start(bf16[1,1,512,1024]{3,2,1,0:T(8,128)(2,1)} %param.19) | copy-start | bytes 3145732
  6.5 2.7 %copy-start.9 = (s32[1,2,1,256,1]{3,4,2,1,0:T(1,128)S(1)}, s32[1,2,1,256,1]{3,4,2,1,0:T(1,128)}, u32[]{:S(2)}) copy-start(s32[1,2,1,256,1]{3,4,2,1,0:T(1,128)} %param.12) | copy-start | bytes 6148
  6.5 5.9 %copy-start.3 = (bf16[1,1,256,1024]{3,2,1,0:T(8,128)(2,1)S(1)}, bf16[1,1,256,1024]{3,2,1,0:T(8,128)(2,1)}, u32[]{:S(2)}) copy-start(bf16[1,1,256,1024]{3,2,1,0:T(8,128)(2,1)} %param.10) | copy-start | bytes 1572868
  6.5 50.6 %all-gather.5.cloned.1.call-start = ((), (), s32[]{:S(2)}) async-start(), calls=%async_computation.4 | async-start | bytes 3932160 | tf_op jit(solution)/shard_map/all_gather | solution.py:130
  7.3 73.9 %all-gather.7.cloned.1.call-start = ((), (), s32[]{:S(2)}) async-start(), calls=%async_computation.5 | async-start | bytes 1310720 | tf_op jit(solution)/shard_map/all_gather | solution.py:131
  8.0 109.2 %all-gather.9.cloned.1.call-start = ((), (), s32[]{:S(2)}) async-start(), calls=%async_computation.6 | async-start | bytes 5242880 | tf_op jit(solution)/shard_map/all_gather | solution.py:135
  8.8 4.4 %collective-permute-start = (bf16[1,512,1024]{2,1,0:T(8,128)(2,1)S(1)}, bf16[1,512,1024]{2,1,0:T(8,128)(2,1)S(1)}, u32[]{:S(2)}, u32[]{:S(2)}) collective-permute-start(bf16[1,512,1024]{2,1,0:T(8,128)(2,1)S(1)} %bitcast.211), channel_id=1, source_target_pairs={{0,4},{4,0},{8,12},{12,8},{1,5},{5,1},{9,13},{13,9},{2,6},{6,2},{1... | collective-permute-start | bytes 3145736 | tf_op jit(solution)/shard_map/ppermute | solution.py:16
  13.1 44.0 %copy-start.11 = (f32[1,1024]{1,0:T(1,128)S(1)}, f32[1,1024]{1,0:T(1,128)}, u32[]{:S(2)}) copy-start(f32[1,1024]{1,0:T(1,128)} %param.13) | copy-start | bytes 12292
  15.6 76.2 %collective-permute-start.1 = (bf16[1,1024,1024]{2,1,0:T(8,128)(2,1)}, bf16[1,1024,1024]{2,1,0:T(8,128)(2,1)}, u32[]{:S(2)}, u32[]{:S(2)}) collective-permute-start(bf16[1,1024,1024]{2,1,0:T(8,128)(2,1)} %maximum_select_fusion.2), channel_id=1, source_target_pairs={{0,8},{4,12},{8,0},{12,4},{1,9},{5,13},{9,1},{13,5},{2,10},{6,14},... | collective-permute-start | bytes 6291464 | tf_op jit(solution)/shard_map/ppermute | solution.py:16
  61.3 1.9 %copy-start.6 = (bf16[256,1536]{0,1:T(8,128)(2,1)S(1)}, bf16[256,1536]{0,1:T(8,128)(2,1)}, u32[]{:S(2)}) copy-start(bf16[256,1536]{0,1:T(8,128)(2,1)} %copy.33) | copy-start | bytes 2359300
  65.0 18.3 %copy-start.8 = (f32[1,1024]{1,0:T(1,128)S(1)}, f32[1,1024]{1,0:T(1,128)}, u32[]{:S(2)}) copy-start(f32[1,1024]{1,0:T(1,128)} %param.16) | copy-start | bytes 12292
  84.6 10.9 %all-to-all-start = ((bf16[1,4,16,1024]{3,2,0,1:T(8,128)(2,1)}), bf16[1,4,16,1024]{3,2,0,1:T(8,128)(2,1)S(1)}, u32[]{:S(2)}, u32[]{:S(2)}) async-start(bf16[1,4,16,1024]{3,2,0,1:T(8,128)(2,1)} %bitcast.22), calls=%async_computation | async-start | bytes 262144 | tf_op jit(solution)/shard_map/all_to_all | solution.py:96
  117.2 33.0 %copy-start.7 = (bf16[1,256,1024]{2,1,0:T(8,128)(2,1)S(1)}, bf16[1,256,1024]{2,1,0:T(8,128)(2,1)}, u32[]{:S(2)}) copy-start(bf16[1,256,1024]{2,1,0:T(8,128)(2,1)} %param.11) | copy-start | bytes 1572868
  125.7 10.9 %all-to-all-start.1 = ((bf16[4,1,16,1024]{3,2,1,0:T(8,128)(2,1)}), bf16[4,1,16,1024]{3,2,1,0:T(8,128)(2,1)S(1)}, u32[]{:S(2)}, u32[]{:S(2)}) async-start(bf16[4,1,16,1024]{3,2,1,0:T(8,128)(2,1)} %bitcast.30), calls=%async_computation.1 | async-start | bytes 262144 | tf_op jit(solution)/shard_map/all_to_all | solution.py:102
  136.6 14.2 %copy-start.10 = (bf16[1,1024,1536]{2,1,0:T(8,128)(2,1)S(1)}, bf16[1,1024,1536]{2,1,0:T(8,128)(2,1)}, u32[]{:S(2)}) copy-start(bf16[1,1024,1536]{2,1,0:T(8,128)(2,1)} %all-gather.5.cloned.1.call-done) | copy-start | bytes 9437188
  137.0 15.0 %copy-start.4 = (bf16[256,1024]{1,0:T(8,128)(2,1)}, bf16[256,1024]{1,0:T(8,128)(2,1)S(1)}, u32[]{:S(2)}) copy-start(bf16[256,1024]{1,0:T(8,128)(2,1)S(1)} %fusion.20) | copy-start | bytes 1572868
  137.0 13.3 %collective-permute-start.2 = (bf16[1,256,1024]{2,1,0:T(8,128)(2,1)S(1)}, bf16[1,256,1024]{2,1,0:T(8,128)(2,1)S(1)}, u32[]{:S(2)}, u32[]{:S(2)}) collective-permute-start(bf16[1,256,1024]{2,1,0:T(8,128)(2,1)S(1)} %bitcast.215), channel_id=1, source_target_pairs={{0,16},{1,17},{2,18},{3,19},{4,20},{5,21},{6,22},{7,23},{8,24},{9,... | collective-permute-start | bytes 1572872 | tf_op jit(solution)/shard_map/ppermute | solution.py:27
  155.9 11.3 %copy-start.2 = (bf16[1024,1024]{1,0:T(8,128)(2,1)S(1)}, bf16[1024,1024]{1,0:T(8,128)(2,1)}, u32[]{:S(2)}) copy-start(bf16[1024,1024]{1,0:T(8,128)(2,1)} %maximum_select_fusion.1) | copy-start | bytes 6291460
  157.4 9.8 %all-to-all-start.2 = ((bf16[1,4,16,1024]{3,2,0,1:T(8,128)(2,1)}), bf16[1,4,16,1024]{3,2,0,1:T(8,128)(2,1)S(1)}, u32[]{:S(2)}, u32[]{:S(2)}) async-start(bf16[1,4,16,1024]{3,2,0,1:T(8,128)(2,1)} %bitcast.51), calls=%async_computation.2 | async-start | bytes 262144 | tf_op jit(solution)/shard_map/all_to_all | solution.py:96
  167.2 16.8 %copy-start.5 = (bf16[256,1024]{1,0:T(8,128)(2,1)S(1)}, bf16[256,1024]{1,0:T(8,128)(2,1)}, u32[]{:S(2)}) copy-start(bf16[256,1024]{1,0:T(8,128)(2,1)} %copy-done.4) | copy-start | bytes 1572868
  174.5 9.2 %all-to-all-start.3 = ((bf16[4,1,16,1024]{3,2,1,0:T(8,128)(2,1)}), bf16[4,1,16,1024]{3,2,1,0:T(8,128)(2,1)S(1)}, u32[]{:S(2)}, u32[]{:S(2)}) async-start(bf16[4,1,16,1024]{3,2,1,0:T(8,128)(2,1)} %bitcast.54), calls=%async_computation.3 | async-start | bytes 262144 | tf_op jit(solution)/shard_map/all_to_all | solution.py:102
Sparse Core Ops, SparseCore 0:
  8.9 48.1 all-gather.4
  58.7 22.3 all-gather.6
  82.7 34.4 all-gather.8
